TPU v7x, 32 devices: a whole 2x2x4 slice. The times are simulated.
32 devices in a mesh: grp: 2 (over y), sx: 4 (over x, core), sy: 4 (over z).
Axes of the slice: x: 2, y: 2, z: 4, core: 2. Of those that a mesh axis runs over, the one named last changes fastest.
Arguments:
- probes: float32 [64, 16, 8, 128], P('grp', 'sx', 'sy'), parts along dimension 0, may hold values from -6 to 6
- lowrank_factor: bfloat16 [32, 8, 128, 4096], P(('grp', 'sx'), 'sy'), parts along dimension 0, may hold values from -0.09375 to 0.09375
- taper_blocks: bfloat16 [32, 8, 5, 128, 128], P(('grp', 'sx'), 'sy'), parts along dimension 0, may hold values from -0.03515625 to 0.03515625
- taper_mask: int32 [32, 8, 5], P(('grp', 'sx'), 'sy'), parts along dimension 0, may hold values 0 or 1
- nugget: float32 [32, 8, 128], P(('grp', 'sx'), 'sy'), parts along dimension 0, may hold values from 1.5 to 6
Outputs:
- solution: float32 [64, 16, 8, 128], P('grp', 'sx', 'sy'), parts along dimension 0
- remainder: float32 [64, 16, 8, 128], P('grp', 'sx', 'sy'), parts along dimension 0
- gradient: float32 [2], P('grp'), parts along dimension 0
There are 2 independent parts, one for each index of `grp`. A program takes and returns all parts, laid end to end along the dimension named above; each array names one. Nothing has to cross between parts.
All inputs are finite; a program needn't handle non-finite values. No bound on the sum of `taper_mask` on one device may be relied on, other than what follows from the above.
Results may differ from a plain program's by a relative error of at most 0.0061.
Values may be sent and summed in bfloat16 or wider, within the bound.
A program may use at most 64 MiB of HBM per device.

v0:
```python
import jax
import jax.numpy as jnp
from jax import lax
from jax.sharding import PartitionSpec as P

ITERS = 2


OFFSETS = ((0, 0), (0, 1), (-1, 0), (1, 1), (1, -1))
HIGH = lax.Precision.HIGHEST


def padded_2(cells, sides, width):
    for axis, dim in sides:
        count = lax.axis_size(axis)
        ends = count - 1
        head = lax.slice_in_dim(cells, 0, width, axis=dim)
        tail = lax.slice_in_dim(cells, cells.shape[dim] - width, cells.shape[dim], axis=dim)
        cells = jnp.concatenate(
            [
                lax.ppermute(tail, axis, [(i, (i + 1) % count) for i in range(ends)]),
                cells,
                lax.ppermute(head, axis, [((i + 1) % count, i) for i in range(ends)]),
            ],
            axis=dim,
        )
    return cells


def sparse_image(direction, narrow, masked, nugget):
    tile_rows = narrow.shape[1]
    tile_cols = narrow.shape[2]
    padded = padded_2(narrow, (("sx", 1), ("sy", 2)), 1)
    beside_all = jnp.stack(
        [
            padded[
                :,
                1 + step_row : 1 + step_row + tile_rows,
                1 + step_col : 1 + step_col + tile_cols,
                :,
            ]
            for step_row, step_col in OFFSETS
        ]
    )
    forward = jnp.einsum(
        "abost,okabt->kabs", masked, beside_all, preferred_element_type=jnp.float32
    )
    backward = jnp.einsum("abost,kabs->okabt", masked, narrow, preferred_element_type=jnp.float32)
    arrived = padded_2(backward[1:].astype(jnp.bfloat16), (("sx", 2), ("sy", 3)), 1).astype(
        jnp.float32
    )
    summed = forward + backward[0]
    for position in range(4):
        step_row, step_col = OFFSETS[position + 1]
        summed = (
            summed
            + arrived[
                position,
                :,
                1 - step_row : 1 - step_row + tile_rows,
                1 - step_col : 1 - step_col + tile_cols,
                :,
            ]
        )
    return summed + nugget[None] * direction


def residual_gram(flat_rem):
    return lax.psum(jnp.dot(flat_rem, flat_rem.T, precision=HIGH), ("sx", "sy"))


def small_solve(matrix, right):
    lower = jnp.linalg.cholesky(matrix)
    return jax.scipy.linalg.cho_solve((lower, True), right)


def local(probes, lowrank_factor, taper_blocks, taper_mask, nugget):
    count = probes.shape[0]
    width = lowrank_factor.shape[-1]
    factor_flat = lowrank_factor.reshape(-1, width)
    shape = probes.shape
    masked = taper_blocks * taper_mask.astype(jnp.bfloat16)[..., None, None]
    solution = jnp.zeros(shape, jnp.float32)
    remainder = probes
    direction = probes
    gram_now = residual_gram(remainder.reshape(count, -1))
    projected = None
    probe_image = None
    for sweep in range(ITERS):
        narrow = direction.astype(jnp.bfloat16)
        image = sparse_image(direction, narrow, masked, nugget)
        flat_dir = direction.reshape(count, -1)
        partial_proj = jnp.dot(
            narrow.reshape(count, -1), factor_flat, preferred_element_type=jnp.float32
        )
        sparse_part = jnp.dot(flat_dir, image.reshape(count, -1).T, precision=HIGH)
        lowrank, sparse_total = lax.psum((partial_proj, sparse_part), ("sx", "sy"))
        curvature = jnp.dot(lowrank, lowrank.T, precision=HIGH) + sparse_total
        lowrank_narrow = lowrank.astype(jnp.bfloat16)
        if sweep == 0:
            probe_image = lowrank
            projected = jnp.zeros(lowrank.shape, jnp.float32)
        image = image + jnp.dot(
            lowrank_narrow, factor_flat.T, preferred_element_type=jnp.float32
        ).reshape(shape)
        step_size = small_solve(curvature, gram_now)
        solution = solution + jnp.dot(step_size.T, flat_dir, precision=HIGH).reshape(shape)
        remainder = remainder - jnp.dot(
            step_size.T, image.reshape(count, -1), precision=HIGH
        ).reshape(shape)
        projected = projected + jnp.dot(step_size.T, lowrank, precision=HIGH)
        if sweep + 1 < ITERS:
            gram_next = residual_gram(remainder.reshape(count, -1))
            mixing = small_solve(gram_now, gram_next)
            direction = remainder + jnp.dot(mixing.T, flat_dir, precision=HIGH).reshape(shape)
            gram_now = gram_next
    total = jnp.sum(projected * probe_image)
    gradient = (total / (count * width)).reshape(1)
    return (solution, remainder, gradient)


def solution(mesh):
    in_specs = (
        P("grp", "sx", "sy", None),
        P(("grp", "sx"), "sy", None, None),
        P(("grp", "sx"), "sy", None, None, None),
        P(("grp", "sx"), "sy", None),
        P(("grp", "sx"), "sy", None),
    )
    out_specs = (P("grp", "sx", "sy", None), P("grp", "sx", "sy", None), P("grp"))
    return jax.shard_map(local, mesh=mesh, in_specs=in_specs, out_specs=out_specs, check_vma=False)
```

profile of v0, /device:TPU:0, one launch (start us, length us, event | category | flops | bytes accessed | tf_op | source)
XLA Modules:
  0.0 340.2 jit_solution(481528040589215053)
XLA Ops:
  7.2 1.6 bitcast_dynamic-update-slice_fusion
  10.1 3.0 collective-permute-start
  13.8 1.7 fusion.76
  16.9 5.2 %collective-permute-start.4 = (bf16[4,32,1,2,128]{4,1,3,2,0:T(8,128)(2,1)S(1)}, bf16[4,32,1,2,128]{4,1,3,2,0:T(8,128)(2,1)S(1)}, u32[]{:S(2)}, u32[]{:S(2)}) collective-permute-start(bf16[4,32,1,2,128]{4,1,3,2,0:T(8,128)(2,1)S(1)} %get-tuple-element.23), channel_id=1, source_target_pairs={{0,4},{4,8},{8,12},{1,5},{5,9},{9,13},{2,6},{6,10},{10,14},{3,7},{... | collective-permute-start | bytes 196616 | tf_op jit(solution)/shard_map/ppermute | solution.py:21
  22.1 5.7 %convolution_bitcast_fusion.1 = f32[32,4096]{1,0:T(8,128)} fusion(bf16[32,4,2,128]{3,0,2,1:T(8,128)(2,1)S(1)} %get-tuple-element.16, bf16[4,2,128,4096]{3,2,1,0:T(8,128)(2,1)} %param.9), kind=kOutput, calls=%fused_computation.3 | convolution fusion | flops 268435456 | bytes 8978432 | tf_op jit(solution)/shard_map/dot_general | solution.py:93
  28.5 1.4 collective-permute-start.2
  30.0 4.5 %collective-permute-start.3 = (bf16[32,6,1,128]{3,0,2,1:T(8,128)(2,1)S(1)}, bf16[32,6,1,128]{3,0,2,1:T(8,128)(2,1)S(1)}, u32[]{:S(2)}, u32[]{:S(2)}) collective-permute-start(bf16[32,6,1,128]{3,0,2,1:T(8,128)(2,1)S(1)} %get-tuple-element.27), channel_id=1, source_target_pairs={{0,1},{1,2},{2,3},{4,5},{5,6},{6,7},{8,9},{9,10},{10,11},{12,13},{... | collective-permute-start | bytes 147464 | tf_op jit(solution)/shard_map/ppermute | solution.py:21
  35.9 4.6 %collective-permute-start.6 = (bf16[4,32,6,1,128]{4,1,3,2,0:T(8,128)(2,1)S(1)}, bf16[4,32,6,1,128]{4,1,3,2,0:T(8,128)(2,1)S(1)}, u32[]{:S(2)}, u32[]{:S(2)}) collective-permute-start(bf16[4,32,6,1,128]{4,1,3,2,0:T(8,128)(2,1)S(1)} %get-tuple-element.19), channel_id=1, source_target_pairs={{0,1},{1,2},{2,3},{4,5},{5,6},{6,7},{8,9},{9,10},{10,11},{12,13},{... | collective-permute-start | bytes 589832 | tf_op jit(solution)/shard_map/ppermute | solution.py:21
  43.2 1.8 collective-permute-done.7
  46.4 1.6 fusion.10
  48.2 60.5 %all-reduce = (f32[32,32]{0,1:T(8,128)S(1)}, f32[32,32]{0,1:T(8,128)S(1)}) all-reduce(f32[32,32]{0,1:T(8,128)S(1)} %convolution_bitcast_fusion.8, f32[32,32]{0,1:T(8,128)S(1)} %convolution_bitcast_fusion.9), channel_id=1, replica_groups=mesh['grp'=2,'sx'=4,'sy'=4] {'sx','sy'}, use_global_device_ids=true, to_apply=%region_4.6 | all-reduce | flops 2048 | bytes 16384 | tf_op jit(solution)/shard_map/psum | solution.py:69
  108.7 11.8 %all-reduce.4.cloned.1.call-done = f32[32,4096]{1,0:T(8,128)} async-done(((f32[32,4096]{1,0:T(8,128)}), f32[32,4096]{1,0:T(8,128)}) %all-reduce.4.cloned.1.call-update) | async-done | bytes 524304 | tf_op jit(solution)/shard_map/psum | solution.py:97
  120.5 1.8 convolution_add_fusion.6
  122.4 2.9 cholesky.59
  126.7 2.4 custom-call.9
  129.6 6.0 %convolution_add_fusion.2 = f32[32,4,2,128]{3,0,2,1:T(8,128)S(1)} fusion(f32[32,4,2,128]{3,0,2,1:T(8,128)S(1)} %fusion.10, bf16[4,2,128,4096]{3,2,1,0:T(8,128)(2,1)} %param.9, f32[32,4096]{1,0:T(8,128)S(1)} %copy-done), kind=kOutput, calls=%fused_computation.11 | convolution fusion | flops 268599296 | bytes 9175040 | tf_op jit(solution)/shard_map/dot_general | solution.py:103
  136.8 60.7 %psum.45 = f32[32,32]{1,0:T(8,128)S(1)} all-reduce(f32[32,32]{1,0:T(8,128)S(1)} %convolution_bitcast_fusion.7), channel_id=1, replica_groups=mesh['grp'=2,'sx'=4,'sy'=4] {'sx','sy'}, use_global_device_ids=true, to_apply=%region_5.0 | all-reduce | flops 1024 | bytes 8192 | tf_op jit(solution)/shard_map/psum | solution.py:69
  197.5 2.9 cholesky.70
  201.7 2.4 custom-call.10
  207.4 5.8 %convolution_bitcast_fusion = f32[32,4096]{1,0:T(8,128)} fusion(bf16[32,4,2,128]{3,0,2,1:T(8,128)(2,1)S(1)} %get-tuple-element.14, bf16[4,2,128,4096]{3,2,1,0:T(8,128)(2,1)} %param.9), kind=kOutput, calls=%fused_computation.2 | convolution fusion | flops 268435456 | bytes 8978432 | tf_op jit(solution)/shard_map/dot_general | solution.py:93
  214.5 3.0 collective-permute-start.8
  220.5 3.0 collective-permute-start.12
  225.0 4.5 %collective-permute-start.11 = (bf16[32,6,1,128]{3,0,2,1:T(8,128)(2,1)S(1)}, bf16[32,6,1,128]{3,0,2,1:T(8,128)(2,1)S(1)}, u32[]{:S(2)}, u32[]{:S(2)}) collective-permute-start(bf16[32,6,1,128]{3,0,2,1:T(8,128)(2,1)S(1)} %get-tuple-element.25), channel_id=1, source_target_pairs={{0,1},{1,2},{2,3},{4,5},{5,6},{6,7},{8,9},{9,10},{10,11},{12,13},{... | collective-permute-start | bytes 147464 | tf_op jit(solution)/shard_map/ppermute | solution.py:21
  229.7 1.5 collective-permute-start.15
  231.2 4.4 %collective-permute-start.14 = (bf16[4,32,6,1,128]{4,1,3,2,0:T(8,128)(2,1)S(1)}, bf16[4,32,6,1,128]{4,1,3,2,0:T(8,128)(2,1)S(1)}, u32[]{:S(2)}, u32[]{:S(2)}) collective-permute-start(bf16[4,32,6,1,128]{4,1,3,2,0:T(8,128)(2,1)S(1)} %get-tuple-element.17), channel_id=1, source_target_pairs={{0,1},{1,2},{2,3},{4,5},{5,6},{6,7},{8,9},{9,10},{10,11},{12,13},{... | collective-permute-start | bytes 589832 | tf_op jit(solution)/shard_map/ppermute | solution.py:21
  236.3 3.8 %collective-permute-done.15 = bf16[4,32,6,1,128]{4,1,3,2,0:T(8,128)(2,1)S(1)} collective-permute-done((bf16[4,32,6,1,128]{4,1,3,2,0:T(8,128)(2,1)S(1)}, bf16[4,32,6,1,128]{4,1,3,2,0:T(8,128)(2,1)S(1)}, u32[]{:S(2)}, u32[]{:S(2)}) %collective-permute-start.15) | collective-permute-done | bytes 196640 | tf_op jit(solution)/shard_map/ppermute | solution.py:23
  242.4 60.4 %psum.47 = f32[32,32]{0,1:T(8,128)S(1)} all-reduce(f32[32,32]{0,1:T(8,128)S(1)} %convolution_bitcast_fusion.5), channel_id=1, replica_groups=mesh['grp'=2,'sx'=4,'sy'=4] {'sx','sy'}, use_global_device_ids=true, to_apply=%region_7.10 | all-reduce | flops 1024 | bytes 8192 | tf_op jit(solution)/shard_map/psum | solution.py:97
  302.8 10.0 %all-reduce.6.cloned.1.call-done = f32[32,4096]{1,0:T(8,128)} async-done(((f32[32,4096]{1,0:T(8,128)}), f32[32,4096]{1,0:T(8,128)}) %all-reduce.6.cloned.1.call-update) | async-done | bytes 524304 | tf_op jit(solution)/shard_map/psum | solution.py:97
  312.8 1.8 convolution_add_fusion.5
  314.7 2.9 cholesky.81
  319.0 2.4 custom-call.11
  322.9 6.0 %convolution_add_fusion.1 = f32[32,4,2,128]{3,0,2,1:T(8,128)S(1)} fusion(f32[32,4,2,128]{3,0,2,1:T(8,128)S(1)} %fusion.19, bf16[4,2,128,4096]{3,2,1,0:T(8,128)(2,1)} %param.9, f32[32,4096]{1,0:T(8,128)S(1)} %copy-done.1), kind=kOutput, calls=%fused_computation.10 | convolution fusion | flops 268599296 | bytes 9175040 | tf_op jit(solution)/shard_map/dot_general | solution.py:103
  (107 shorter events, 31.4 us)
Async XLA Ops:
  7.2 113.3 %all-reduce.4.cloned.1.call-start = ((), (), s32[]{:S(2)}) async-start(), calls=%async_computation | async-start | bytes 1048576 | tf_op jit(solution)/shard_map/psum | solution.py:97
  8.8 19.7 %collective-permute-start.1 = (bf16[32,1,2,128]{3,0,2,1:T(8,128)(2,1)S(1)}, bf16[32,1,2,128]{3,0,2,1:T(8,128)(2,1)S(1)}, u32[]{:S(2)}, u32[]{:S(2)}) collective-permute-start(bf16[32,1,2,128]{3,0,2,1:T(8,128)(2,1)S(1)} %get-tuple-element.32), channel_id=1, source_target_pairs={{4,0},{8,4},{12,8},{5,1},{9,5},{13,9},{6,2},{10,6},{14,10},{7,3},{... | collective-permute-start | bytes 49160 | tf_op jit(solution)/shard_map/ppermute | solution.py:23
  10.1 18.4 %collective-permute-start = (bf16[32,1,2,128]{3,0,2,1:T(8,128)(2,1)S(1)}, bf16[32,1,2,128]{3,0,2,1:T(8,128)(2,1)S(1)}, u32[]{:S(2)}, u32[]{:S(2)}) collective-permute-start(bf16[32,1,2,128]{3,0,2,1:T(8,128)(2,1)S(1)} %get-tuple-element.31), channel_id=1, source_target_pairs={{0,4},{4,8},{8,12},{1,5},{5,9},{9,13},{2,6},{6,10},{10,14},{3,7},{... | collective-permute-start | bytes 49160 | tf_op jit(solution)/shard_map/ppermute | solution.py:21
  15.6 19.0 %collective-permute-start.5 = (bf16[4,32,1,2,128]{4,1,3,2,0:T(8,128)(2,1)S(1)}, bf16[4,32,1,2,128]{4,1,3,2,0:T(8,128)(2,1)S(1)}, u32[]{:S(2)}, u32[]{:S(2)}) collective-permute-start(bf16[4,32,1,2,128]{4,1,3,2,0:T(8,128)(2,1)S(1)} %get-tuple-element.24), channel_id=1, source_target_pairs={{4,0},{8,4},{12,8},{5,1},{9,5},{13,9},{6,2},{10,6},{14,10},{7,3},{... | collective-permute-start | bytes 196616 | tf_op jit(solution)/shard_map/ppermute | solution.py:23
  16.9 11.0 %copy-start.3 = (f32[32,4,2,128]{3,2,1,0:T(2,128)S(1)}, f32[32,4,2,128]{3,2,1,0:T(2,128)}, u32[]{:S(2)}) copy-start(f32[32,4,2,128]{3,2,1,0:T(2,128)} %param.8) | copy-start | bytes 393220
  16.9 17.6 %collective-permute-start.4 = (bf16[4,32,1,2,128]{4,1,3,2,0:T(8,128)(2,1)S(1)}, bf16[4,32,1,2,128]{4,1,3,2,0:T(8,128)(2,1)S(1)}, u32[]{:S(2)}, u32[]{:S(2)}) collective-permute-start(bf16[4,32,1,2,128]{4,1,3,2,0:T(8,128)(2,1)S(1)} %get-tuple-element.23), channel_id=1, source_target_pairs={{0,4},{4,8},{8,12},{1,5},{5,9},{9,13},{2,6},{6,10},{10,14},{3,7},{... | collective-permute-start | bytes 196616 | tf_op jit(solution)/shard_map/ppermute | solution.py:21
  27.9 284.9 %all-reduce.6.cloned.1.call-start = ((), (), s32[]{:S(2)}) async-start(), calls=%async_computation.1 | async-start | bytes 1048576 | tf_op jit(solution)/shard_map/psum | solution.py:97
  28.5 17.9 %copy-start.2 = (bf16[4,2,5,128,128]{4,3,2,1,0:T(8,128)(2,1)S(1)}, bf16[4,2,5,128,128]{4,3,2,1,0:T(8,128)(2,1)}, u32[]{:S(2)}) copy-start(bf16[4,2,5,128,128]{4,3,2,1,0:T(8,128)(2,1)} %param.10) | copy-start | bytes 3932164
  28.5 17.8 %copy-start.5 = (f32[4,2,128]{2,1,0:T(2,128)S(1)}, f32[4,2,128]{2,1,0:T(2,128)}, u32[]{:S(2)}) copy-start(f32[4,2,128]{2,1,0:T(2,128)} %param.12) | copy-start | bytes 12292
  28.5 12.0 %collective-permute-start.2 = (bf16[32,6,1,128]{3,0,2,1:T(8,128)(2,1)S(1)}, bf16[32,6,1,128]{3,0,2,1:T(8,128)(2,1)S(1)}, u32[]{:S(2)}, u32[]{:S(2)}) collective-permute-start(bf16[32,6,1,128]{3,0,2,1:T(8,128)(2,1)S(1)} %get-tuple-element.28), channel_id=1, source_target_pairs={{1,0},{2,1},{3,2},{5,4},{6,5},{7,6},{9,8},{10,9},{11,10},{13,12},{... | collective-permute-start | bytes 147464 | tf_op jit(solution)/shard_map/ppermute | solution.py:23
  30.0 12.5 %collective-permute-start.3 = (bf16[32,6,1,128]{3,0,2,1:T(8,128)(2,1)S(1)}, bf16[32,6,1,128]{3,0,2,1:T(8,128)(2,1)S(1)}, u32[]{:S(2)}, u32[]{:S(2)}) collective-permute-start(bf16[32,6,1,128]{3,0,2,1:T(8,128)(2,1)S(1)} %get-tuple-element.27), channel_id=1, source_target_pairs={{0,1},{1,2},{2,3},{4,5},{5,6},{6,7},{8,9},{9,10},{10,11},{12,13},{... | collective-permute-start | bytes 147464 | tf_op jit(solution)/shard_map/ppermute | solution.py:21
  34.6 10.4 %collective-permute-start.7 = (bf16[4,32,6,1,128]{4,1,3,2,0:T(8,128)(2,1)S(1)}, bf16[4,32,6,1,128]{4,1,3,2,0:T(8,128)(2,1)S(1)}, u32[]{:S(2)}, u32[]{:S(2)}) collective-permute-start(bf16[4,32,6,1,128]{4,1,3,2,0:T(8,128)(2,1)S(1)} %get-tuple-element.20), channel_id=1, source_target_pairs={{1,0},{2,1},{3,2},{5,4},{6,5},{7,6},{9,8},{10,9},{11,10},{13,12},{... | collective-permute-start | bytes 589832 | tf_op jit(solution)/shard_map/ppermute | solution.py:23
  35.9 10.4 %collective-permute-start.6 = (bf16[4,32,6,1,128]{4,1,3,2,0:T(8,128)(2,1)S(1)}, bf16[4,32,6,1,128]{4,1,3,2,0:T(8,128)(2,1)S(1)}, u32[]{:S(2)}, u32[]{:S(2)}) collective-permute-start(bf16[4,32,6,1,128]{4,1,3,2,0:T(8,128)(2,1)S(1)} %get-tuple-element.19), channel_id=1, source_target_pairs={{0,1},{1,2},{2,3},{4,5},{5,6},{6,7},{8,9},{9,10},{10,11},{12,13},{... | collective-permute-start | bytes 589832 | tf_op jit(solution)/shard_map/ppermute | solution.py:21
  120.5 9.1 %copy-start = (f32[32,4096]{1,0:T(8,128)S(1)}, f32[32,4096]{1,0:T(8,128)}, u32[]{:S(2)}) copy-start(f32[32,4096]{1,0:T(8,128)} %all-reduce.4.cloned.1.call-done) | copy-start | bytes 1572868
  213.2 10.4 %collective-permute-start.9 = (bf16[32,1,2,128]{3,0,2,1:T(8,128)(2,1)}, bf16[32,1,2,128]{3,0,2,1:T(8,128)(2,1)S(1)}, u32[]{:S(2)}, u32[]{:S(2)}) collective-permute-start(bf16[32,1,2,128]{3,0,2,1:T(8,128)(2,1)} %get-tuple-element.30), channel_id=1, source_target_pairs={{4,0},{8,4},{12,8},{5,1},{9,5},{13,9},{6,2},{10,6},{14,10},{7,3},{... | collective-permute-start | bytes 49160 | tf_op jit(solution)/shard_map/ppermute | solution.py:23
  214.5 9.1 %collective-permute-start.8 = (bf16[32,1,2,128]{3,0,2,1:T(8,128)(2,1)S(1)}, bf16[32,1,2,128]{3,0,2,1:T(8,128)(2,1)S(1)}, u32[]{:S(2)}, u32[]{:S(2)}) collective-permute-start(bf16[32,1,2,128]{3,0,2,1:T(8,128)(2,1)S(1)} %get-tuple-element.29), channel_id=1, source_target_pairs={{0,4},{4,8},{8,12},{1,5},{5,9},{9,13},{2,6},{6,10},{10,14},{3,7},{... | collective-permute-start | bytes 49160 | tf_op jit(solution)/shard_map/ppermute | solution.py:21
  219.2 10.4 %collective-permute-start.13 = (bf16[4,32,1,2,128]{4,1,3,2,0:T(8,128)(2,1)}, bf16[4,32,1,2,128]{4,1,3,2,0:T(8,128)(2,1)S(1)}, u32[]{:S(2)}, u32[]{:S(2)}) collective-permute-start(bf16[4,32,1,2,128]{4,1,3,2,0:T(8,128)(2,1)} %get-tuple-element.22), channel_id=1, source_target_pairs={{4,0},{8,4},{12,8},{5,1},{9,5},{13,9},{6,2},{10,6},{14,10},{7,3},{... | collective-permute-start | bytes 196616 | tf_op jit(solution)/shard_map/ppermute | solution.py:23
  220.5 9.1 %collective-permute-start.12 = (bf16[4,32,1,2,128]{4,1,3,2,0:T(8,128)(2,1)}, bf16[4,32,1,2,128]{4,1,3,2,0:T(8,128)(2,1)S(1)}, u32[]{:S(2)}, u32[]{:S(2)}) collective-permute-start(bf16[4,32,1,2,128]{4,1,3,2,0:T(8,128)(2,1)} %get-tuple-element.21), channel_id=1, source_target_pairs={{0,4},{4,8},{8,12},{1,5},{5,9},{9,13},{2,6},{6,10},{10,14},{3,7},{... | collective-permute-start | bytes 196616 | tf_op jit(solution)/shard_map/ppermute | solution.py:21
  223.5 12.1 %copy-start.4 = (bf16[5,32,4,2,128]{4,1,3,2,0:T(8,128)(2,1)S(1)}, bf16[5,32,4,2,128]{4,1,3,2,0:T(8,128)(2,1)}, u32[]{:S(2)}) copy-start(bf16[5,32,4,2,128]{4,1,3,2,0:T(8,128)(2,1)} %get-tuple-element.13) | copy-start | bytes 983044
  223.6 12.0 %collective-permute-start.10 = (bf16[32,6,1,128]{3,0,2,1:T(8,128)(2,1)S(1)}, bf16[32,6,1,128]{3,0,2,1:T(8,128)(2,1)S(1)}, u32[]{:S(2)}, u32[]{:S(2)}) collective-permute-start(bf16[32,6,1,128]{3,0,2,1:T(8,128)(2,1)S(1)} %get-tuple-element.26), channel_id=1, source_target_pairs={{1,0},{2,1},{3,2},{5,4},{6,5},{7,6},{9,8},{10,9},{11,10},{13,12},{... | collective-permute-start | bytes 147464 | tf_op jit(solution)/shard_map/ppermute | solution.py:23
  225.0 10.6 %collective-permute-start.11 = (bf16[32,6,1,128]{3,0,2,1:T(8,128)(2,1)S(1)}, bf16[32,6,1,128]{3,0,2,1:T(8,128)(2,1)S(1)}, u32[]{:S(2)}, u32[]{:S(2)}) collective-permute-start(bf16[32,6,1,128]{3,0,2,1:T(8,128)(2,1)S(1)} %get-tuple-element.25), channel_id=1, source_target_pairs={{0,1},{1,2},{2,3},{4,5},{5,6},{6,7},{8,9},{9,10},{10,11},{12,13},{... | collective-permute-start | bytes 147464 | tf_op jit(solution)/shard_map/ppermute | solution.py:21
  229.7 10.4 %collective-permute-start.15 = (bf16[4,32,6,1,128]{4,1,3,2,0:T(8,128)(2,1)S(1)}, bf16[4,32,6,1,128]{4,1,3,2,0:T(8,128)(2,1)S(1)}, u32[]{:S(2)}, u32[]{:S(2)}) collective-permute-start(bf16[4,32,6,1,128]{4,1,3,2,0:T(8,128)(2,1)S(1)} %get-tuple-element.18), channel_id=1, source_target_pairs={{1,0},{2,1},{3,2},{5,4},{6,5},{7,6},{9,8},{10,9},{11,10},{13,12},{... | collective-permute-start | bytes 589832 | tf_op jit(solution)/shard_map/ppermute | solution.py:23
  231.2 10.0 %collective-permute-start.14 = (bf16[4,32,6,1,128]{4,1,3,2,0:T(8,128)(2,1)S(1)}, bf16[4,32,6,1,128]{4,1,3,2,0:T(8,128)(2,1)S(1)}, u32[]{:S(2)}, u32[]{:S(2)}) collective-permute-start(bf16[4,32,6,1,128]{4,1,3,2,0:T(8,128)(2,1)S(1)} %get-tuple-element.17), channel_id=1, source_target_pairs={{0,1},{1,2},{2,3},{4,5},{5,6},{6,7},{8,9},{9,10},{10,11},{12,13},{... | collective-permute-start | bytes 589832 | tf_op jit(solution)/shard_map/ppermute | solution.py:21
  312.8 10.1 %copy-start.1 = (f32[32,4096]{1,0:T(8,128)S(1)}, f32[32,4096]{1,0:T(8,128)}, u32[]{:S(2)}) copy-start(f32[32,4096]{1,0:T(8,128)} %all-reduce.6.cloned.1.call-done) | copy-start | bytes 1572868
Sparse Core Ops, SparseCore 0:
  28.0 92.4 all-reduce.3
  223.6 89.1 all-reduce.5
where the time goes:
time: 341 us; the launch traced here: 340 us
  blocking collectives  182 us (53%)
  starting transfers between devices  43.2 us (13%)
  matrix products  38.5 us (11%)
  waiting for transfers between devices  29.9 us (9%)
  other arithmetic  24.6 us (7%)
  between operations  16.4 us (5%)
  local copies, waits for them, and re-layouts  5.94 us (2%)
    psum x2, blocking collectives, residual_gram(): return lax.psum(jnp.dot(flat_rem, flat_rem.T, precision=HIGH), ('sx', 'sy'))  121 us
    psum x1, blocking collectives, local(): lowrank, sparse_total = lax.psum((partial_proj, sparse_part), ('sx', 'sy'))  60.4 us
    ppermute x8, starting transfers between devices, padded_2(): lax.ppermute(tail, axis, [(i, (i + 1) % count) for i in range(ends)])  32.4 us
    psum x2, waiting for transfers between devices, local(): lowrank, sparse_total = lax.psum((partial_proj, sparse_part), ('sx', 'sy'))  21.8 us
    dot_general x2, matrix products, local(): jnp.dot(lowrank_narrow, factor_flat.T, preferred_element_type=jnp.float32)  11.9 us
    dot_general x2, matrix products, local(): jnp.dot(narrow.reshape(count, -1), factor_flat, preferred_element_type=jn...  11.5 us
    another operation x9, other arithmetic, small_solve(): lower = jnp.linalg.cholesky(matrix)  10.8 us
    ppermute x8, starting transfers between devices, padded_2(): lax.ppermute(head, axis, [((i + 1) % count, i) for i in range(ends)])  10.8 us
  transfers between devices with their start and end apart: 18, of which 6 were waited for; matrix products, arithmetic and copies ran while one was open for 5% of the time, Pallas kernels for 0%

commit v1 on v0

v1 whole, which is shorter than its diff:
```python
import functools

import jax
import jax.numpy as jnp
from jax import lax
from jax.experimental import pallas as pl
from jax.experimental.pallas import tpu as pltpu
from jax.sharding import PartitionSpec as P

OFFSETS = ((0, 0), (0, 1), (-1, 0), (1, 1), (1, -1))
HIGH = lax.Precision.HIGHEST
F32 = jnp.float32
BF16 = jnp.bfloat16
CHUNK = 256
NT = (((1,), (1,)), ((), ()))
TN = (((0,), (0,)), ((), ()))
MESH = pl.DeviceIdType.MESH


def side(index, length):
    return -1 if index < 0 else (1 if index >= length else 0)


def halo_plan(rows, cols):
    sends = {}
    for r in range(rows):
        for c in range(cols):
            for o in range(1, 5):
                dr, dc = OFFSETS[o]
                for sign, item in ((-1, ("v", 0, r, c)), (1, ("c", o, r, c))):
                    way = (side(r + sign * dr, rows), side(c + sign * dc, cols))
                    if way != (0, 0) and item not in sends.setdefault(way, []):
                        sends[way].append(item)
    sends = {way: items for way, items in sorted(sends.items()) if items}
    base, total = {}, 0
    for way, items in sends.items():
        base[way] = total
        total += len(items)
    return sends, base, total


def high(a, b, dims):
    return lax.dot_general(a, b, dims, precision=HIGH, preferred_element_type=F32)


def eliminate(matrix, rights):
    size = matrix.shape[0]
    sub = lax.broadcasted_iota(jnp.int32, (size, 1), 0)
    for k in range(size):
        pivot = 1.0 / matrix[k : k + 1, k : k + 1]
        column = matrix[:, k : k + 1]

        def step(array):
            row = array[k : k + 1, :] * pivot
            return jnp.where(sub == k, row, array - column * row)

        rights = [step(right) for right in rights]
        matrix = step(matrix)
    return rights


def kernel(dims, x_ref, f_hbm, b_hbm, mask_ref, nug_ref, sol_ref, rem_ref, grad_ref,
           f_v, b_v, xb, part, own, rs_in, s2_out, s2_in, full, hal_out, hal_in, cprod, sm_out, sm_in, sm2_out, sm2_in,
           f_sem, b_sem, snd, rcv, hs, hr):
    nx, ny, rows, cols, count, width = dims
    tiles = rows * cols
    points = tiles * 128
    piece = width // nx
    pc = piece // CHUNK
    split = pc % ny == 0
    sc = pc // ny if split else pc
    i = lax.axis_index("sx")
    j = lax.axis_index("sy")
    sends, base, _ = halo_plan(rows, cols)
    ways = list(sends)

    def xp(d):
        return {"sx": lax.rem(i + d, nx)}

    def yp(d):
        return {"sy": lax.rem(j + d, ny)}

    def exists(way):
        a, b = i + way[0], j + way[1]
        return (a >= 0) & (a < nx) & (b >= 0) & (b < ny)

    def neighbour(way):
        return {"sx": i + way[0], "sy": j + way[1]}

    f_copies = []
    for d in range(1, nx + 1):
        p = lax.rem(i + d, nx)
        copy = pltpu.make_async_copy(
            f_hbm.at[:, pl.ds(pl.multiple_of(p * piece, piece), piece)], f_v.at[p], f_sem.at[d - 1])
        copy.start()
        f_copies.append(copy)
    b_copy = pltpu.make_async_copy(b_hbm, b_v, b_sem)
    b_copy.start()

    barrier = pltpu.get_barrier_semaphore()
    for d in range(1, nx):
        pl.semaphore_signal(barrier, inc=1, device_id=xp(d), device_id_type=MESH)
    for d in range(1, ny):
        pl.semaphore_signal(barrier, inc=1, device_id=yp(d), device_id_type=MESH)
    corners = [(a, b) for a in (-1, 1) for b in (-1, 1)]
    for way in corners:
        @pl.when(exists(way))
        def _():
            pl.semaphore_signal(barrier, inc=1, device_id=neighbour(way), device_id_type=MESH)
    near = sum(jnp.where(exists(way), 1, 0) for way in corners)
    pl.semaphore_wait(barrier, nx + ny - 2 + near)

    def remote(src, dst, it, slot, target):
        return pltpu.make_async_remote_copy(
            src_ref=src, dst_ref=dst, send_sem=snd.at[it, slot], recv_sem=rcv.at[it, slot],
            device_id=target, device_id_type=MESH)

    def image(it, x):
        narrow = x.astype(BF16)
        xb[it] = narrow
        pend = []
        slot = 0
        st1 = []
        for d in range(1, nx + 1):
            p = lax.rem(i + d, nx)
            if it == 0:
                f_copies[d - 1].wait()
            product = jnp.dot(xb[it], f_v[p], preferred_element_type=F32)
            for c in range(pc):
                piece_c = product[:, c * CHUNK : (c + 1) * CHUNK]
                if d < nx:
                    part[it, p, c] = piece_c.astype(BF16)
                else:
                    own[c] = piece_c
            if d < nx:
                copy = remote(part.at[it, p], rs_in.at[it, d - 1], it, slot, xp(d))
                copy.start()
                st1.append(copy)
                slot += 1
        if it == 0:
            b_copy.wait()

        def block(r, c, o):
            return b_v[pl.ds(((r * cols + c) * 5 + o) * 128, 128), :]

        def tile(r, c):
            t = r * cols + c
            return xb[it, :, t * 128 : (t + 1) * 128]

        def mask(r, c, o):
            return mask_ref[r, c, o].astype(F32)

        order = [(o, r, c) for o in range(1, 5) for r in range(rows) for c in range(cols)]
        for o, r, c in order:
            value = jnp.dot(tile(r, c), block(r, c, o), preferred_element_type=F32) * mask(r, c, o)
            cprod[it, (r * cols + c) * 4 + o - 1] = value.astype(BF16)
        halo = []
        for n, way in enumerate(ways):
            for k, (kind, o, r, c) in enumerate(sends[way]):
                hal_out[it, base[way] + k] = tile(r, c) if kind == "v" else cprod[it, (r * cols + c) * 4 + o - 1]
            span = pl.ds(base[way], len(sends[way]))
            copy = pltpu.make_async_remote_copy(
                src_ref=hal_out.at[it, span], dst_ref=hal_in.at[it, span], send_sem=hs.at[it, n], recv_sem=hr.at[it, n],
                device_id=neighbour(way), device_id_type=MESH)
            back = (-way[0], -way[1])
            halo.append((copy, way, back))

            @pl.when(exists(way))
            def _():
                copy.start()
        for copy in st1:
            copy.wait_recv()
        for c in range(pc):
            total = own[c]
            for d in range(1, nx):
                total = total + rs_in[it, d - 1, c].astype(F32)
            own[c] = total
            s2_out[it, c] = total.astype(BF16)
        st2 = []
        for d in range(1, ny):
            q = lax.rem(j + d, ny)
            src = s2_out.at[it, pl.ds(q * sc, sc)] if split else s2_out.at[it]
            dst = s2_in.at[it, d - 1] if split else s2_in.at[it, j]
            copy = remote(src, dst, it, slot, yp(d))
            copy.start()
            st2.append(copy)
            slot += 1
        for copy, way, back in halo:
            @pl.when(exists(back))
            def _():
                copy.wait_recv()

            @pl.when(jnp.logical_not(exists(back)))
            def _():
                span = pl.ds(base[way], len(sends[way]))
                hal_in[it, span] = jnp.zeros((len(sends[way]), count, 128), BF16)

        def arrived(kind, o, r, c):
            e = (side(r, rows), side(c, cols))
            if e == (0, 0):
                return tile(r, c) if kind == "v" else cprod[it, (r * cols + c) * 4 + o - 1]
            way = (-e[0], -e[1])
            return hal_in[it, base[way] + sends[way].index((kind, o, r - e[0] * rows, c - e[1] * cols))]

        image_tiles = []
        for r in range(rows):
            for c in range(cols):
                t = r * cols + c
                total = nug_ref[t : t + 1, :] * x[:, t * 128 : (t + 1) * 128]
                for o, (dr, dc) in enumerate(OFFSETS):
                    ahead = tile(r, c) if o == 0 else arrived("v", 0, r + dr, c + dc)
                    total = total + mask(r, c, o) * lax.dot_general(ahead, block(r, c, o), NT, preferred_element_type=F32)
                    if o == 0:
                        total = total + mask(r, c, 0) * jnp.dot(ahead, block(r, c, 0), preferred_element_type=F32)
                    else:
                        total = total + arrived("c", o, r - dr, c - dc).astype(F32)
                image_tiles.append(total)
        sparse = jnp.concatenate(image_tiles, axis=1)
        return sparse, slot, st1, st2, halo

    def finish(it, x, sparse, first, state):
        _, slot, st1, st2, halo = state
        for copy in st2:
            copy.wait_recv()
        st3 = []
        if split:
            for c in range(sc):
                total = own[j * sc + c]
                for d in range(1, ny):
                    total = total + s2_in[it, d - 1, c].astype(F32)
                full[it, i * pc + j * sc + c] = total.astype(BF16)
            for d in range(1, ny):
                span = pl.ds(i * pc + j * sc, sc)
                copy = remote(full.at[it, span], full.at[it, span], it, slot, yp(d))
                copy.start()
                st3.append(copy)
                slot += 1
        else:
            for c in range(pc):
                s2_in[it, j, c] = s2_out[it, c]
                total = s2_in[it, 0, c].astype(F32)
                for q in range(1, ny):
                    total = total + s2_in[it, q, c].astype(F32)
                full[it, i * pc + c] = total.astype(BF16)
        grams = high(x, jnp.concatenate([x, sparse, first, first], axis=0), NT)
        sm_out[it] = grams
        sm_in[it, i] = grams
        sm1 = []
        for d in range(1, nx):
            copy = remote(sm_out.at[it], sm_in.at[it, i], it, slot, xp(d))
            copy.start()
            sm1.append(copy)
            slot += 1
        for copy in st3:
            copy.wait_recv()
        st4 = []
        for d in range(1, nx):
            span = pl.ds(i * pc, pc)
            copy = remote(full.at[it, span], full.at[it, span], it, slot, xp(d))
            copy.start()
            st4.append(copy)
            slot += 1
        for copy in sm1:
            copy.wait_recv()
        total = sm_in[it, 0]
        for d in range(1, nx):
            total = total + sm_in[it, d]
        sm2_out[it] = total
        sm2_in[it, j] = total
        sm2 = []
        for d in range(1, ny):
            copy = remote(sm2_out.at[it], sm2_in.at[it, j], it, slot, yp(d))
            copy.start()
            sm2.append(copy)
            slot += 1
        image_total = sparse
        for d in range(nx):
            p = lax.rem(i - d + nx, nx)
            if d:
                st4[d - 1].wait_recv()
            for c in range(pc):
                image_total = image_total + lax.dot_general(
                    full[it, p * pc + c], f_v[p, :, c * CHUNK : (c + 1) * CHUNK], NT, preferred_element_type=F32)
        low = None
        for c in range(width // CHUNK):
            mine = full[it, c]
            both = mine if it == 0 else jnp.concatenate([full[0, c], mine], axis=0)
            term = lax.dot_general(mine, both, NT, preferred_element_type=F32)
            low = term if low is None else low + term
        for copy in sm2:
            copy.wait_recv()
        total = sm2_in[it, 0]
        for d in range(1, ny):
            total = total + sm2_in[it, d]
        for copy in st1 + st2 + st3 + sm1 + st4 + sm2:
            copy.wait_send()
        for copy, way, back in halo:
            @pl.when(exists(way))
            def _():
                copy.wait_send()
        return image_total, low, total

    n = count
    x0 = jnp.concatenate([x_ref[pl.ds(t, n, stride=tiles), :] for t in range(tiles)], axis=1)
    state = image(0, x0)
    y0 = state[0]
    w0, uu, small = finish(0, x0, y0, y0, state)
    g0 = small[:, :n]
    h0 = uu + small[:, n : 2 * n]
    (s0,) = eliminate(h0, [g0])
    r1 = x0 - high(s0, w0, TN)
    state = image(1, r1)
    y1 = state[0]
    t1, low, small = finish(1, r1, y1, y0, state)
    g1 = small[:, :n]
    rar = low[:, n : 2 * n] + small[:, n : 2 * n]
    rav = low[:, :n] + small[:, 2 * n : 3 * n]
    (m,) = eliminate(g0, [g1])
    half = high(rav, m, (((1,), (0,)), ((), ())))
    h1 = rar + half + half.T + high(m, high(h0, m, (((1,), (0,)), ((), ()))), TN)
    (s1,) = eliminate(h1, [g1])
    ms = high(m, s1, (((1,), (0,)), ((), ())))
    answer = high(s0 + ms, x0, TN) + high(s1, r1, TN)
    left = r1 - high(s1, t1, TN) - high(ms, w0, TN)
    for t in range(tiles):
        sol_ref[pl.ds(t, n, stride=tiles), :] = answer[:, t * 128 : (t + 1) * 128]
        rem_ref[pl.ds(t, n, stride=tiles), :] = left[:, t * 128 : (t + 1) * 128]
    trace = (s0 * uu + s1 * (low[:, :n] + high(m, uu, TN))) * (1.0 / (count * width))
    grad_ref[0] = jnp.sum(trace)


def local(nx, ny, probes, lowrank_factor, taper_blocks, taper_mask, nugget):
    count, rows, cols, span = probes.shape
    width = lowrank_factor.shape[-1]
    tiles = rows * cols
    points = tiles * span
    piece = width // nx
    pc = piece // CHUNK
    split = pc % ny == 0
    halo = halo_plan(rows, cols)
    slots = 3 * (nx - 1) + 3 * (ny - 1)
    vm = pltpu.VMEM
    dma = pltpu.SemaphoreType.DMA
    sc = pc // ny if split else pc
    answer, left, gradient = pl.pallas_call(
        functools.partial(kernel, (nx, ny, rows, cols, count, width)),
        out_shape=(
            jax.ShapeDtypeStruct((count * tiles, span), F32),
            jax.ShapeDtypeStruct((count * tiles, span), F32),
            jax.ShapeDtypeStruct((1,), F32),
        ),
        in_specs=[
            pl.BlockSpec(memory_space=vm),
            pl.BlockSpec(memory_space=pl.ANY),
            pl.BlockSpec(memory_space=pl.ANY),
            pl.BlockSpec(memory_space=pltpu.SMEM),
            pl.BlockSpec(memory_space=vm),
        ],
        out_specs=(
            pl.BlockSpec(memory_space=vm),
            pl.BlockSpec(memory_space=vm),
            pl.BlockSpec(memory_space=pltpu.SMEM),
        ),
        scratch_shapes=[
            vm((nx, points, piece), BF16),
            vm((tiles * 5 * span, span), BF16),
            vm((2, count, points), BF16),
            vm((2, nx, pc, count, CHUNK), BF16),
            vm((pc, count, CHUNK), F32),
            vm((2, nx - 1, pc, count, CHUNK), BF16),
            vm((2, pc, count, CHUNK), BF16),
            vm((2, ny - 1 if split else ny, sc, count, CHUNK), BF16),
            vm((2, width // CHUNK, count, CHUNK), BF16),
            vm((2, halo[2], count, span), BF16),
            vm((2, halo[2], count, span), BF16),
            vm((2, tiles * 4, count, span), BF16),
            vm((2, count, 4 * count), F32),
            vm((2, nx, count, 4 * count), F32),
            vm((2, count, 4 * count), F32),
            vm((2, ny, count, 4 * count), F32),
            dma((nx,)),
            dma,
            dma((2, slots)),
            dma((2, slots)),
            dma((2, len(halo[0]))),
            dma((2, len(halo[0]))),
        ],
        compiler_params=pltpu.CompilerParams(
            collective_id=0, has_side_effects=True, vmem_limit_bytes=48 * 1024 * 1024),
    )(
        probes.reshape(count * tiles, span),
        lowrank_factor.reshape(points, width),
        taper_blocks.reshape(tiles * 5 * span, span),
        taper_mask,
        nugget.reshape(tiles, span),
    )
    return answer.reshape(probes.shape), left.reshape(probes.shape), gradient


def solution(mesh):
    in_specs = (
        P("grp", "sx", "sy", None),
        P(("grp", "sx"), "sy", None, None),
        P(("grp", "sx"), "sy", None, None, None),
        P(("grp", "sx"), "sy", None),
        P(("grp", "sx"), "sy", None),
    )
    out_specs = (P("grp", "sx", "sy", None), P("grp", "sx", "sy", None), P("grp"))
    run = functools.partial(local, mesh.shape["sx"], mesh.shape["sy"])
    return jax.shard_map(run, mesh=mesh, in_specs=in_specs, out_specs=out_specs, check_vma=False)
```

time: 341 us -> 62.5 us (0.18)
  blocking collectives: 182 us -> 0 us
  Pallas kernels: 0 us -> 55 us
  starting transfers between devices: 43.2 us -> 0 us
  matrix products: 38.5 us -> 0 us
  waiting for transfers between devices: 29.9 us -> 0 us
  other arithmetic: 24.6 us -> 0 us
  between operations: 16.4 us -> 2.4 us
    psum x3 -> x0, blocking collectives: 182 us -> none  [the longest x2 121 us: residual_gram(): return lax.psum(jnp.dot(flat_rem, flat_rem.T, precision=HIGH), ('sx', 'sy'))]
    pallas_call x0 -> x1, Pallas kernels: none -> 55 us  [local(): pl.pallas_call(functools.partial(kernel, (nx, ny, rows, cols, count, widt...]
    ppermute x16 -> x0, starting transfers between devices: 43.1 us -> none  [the longest x8 32.4 us: padded_2(): lax.ppermute(tail, axis, [(i, (i + 1) % count) for i in range(ends)])]
    dot_general x21 -> x0, matrix products: 37.4 us -> none  [the longest x2 11.9 us: local(): jnp.dot(lowrank_narrow, factor_flat.T, preferred_element_type=jnp.float32)]
    psum x2 -> x0, waiting for transfers between devices: 21.8 us -> none  [local(): lowrank, sparse_total = lax.psum((partial_proj, sparse_part), ('sx', 'sy'))]
    another operation x17 -> x0, other arithmetic: 20.7 us -> none  [the longest x9 10.8 us: small_solve(): lower = jnp.linalg.cholesky(matrix)]
    ppermute x16 -> x0, waiting for transfers between devices: 8.08 us -> none  [the longest x8 5.67 us: padded_2(): lax.ppermute(head, axis, [((i + 1) % count, i) for i in range(ends)])]
  transfers between devices with their start and end apart: 18 -> 0, of which waited for: 6 -> 0; matrix products, arithmetic and copies ran while one was open for 5% -> 0% of each run, Pallas kernels for 0% -> 0%
where the time goes in v1:
time: 62.5 us; the launch traced here: 62.3 us
  Pallas kernels  55 us (88%)
  local copies, waits for them, and re-layouts  4.9 us (8%)
  between operations  2.4 us (4%)
    pallas_call x1, Pallas kernels, local(): pl.pallas_call(functools.partial(kernel, (nx, ny, rows, cols, count, widt...  55 us
    unnamed x10, local copies, waits for them, and re-layouts  4.9 us

profile of v1, /device:TPU:0, one launch (start us, length us, event | category | flops | bytes accessed | tf_op | source)
XLA Modules:
  0.0 62.3 jit_solution(740554486831525895)
XLA Ops:
  0.6 0.0 copy-start
  0.6 1.3 %copy-done = bf16[4,2,5,128,128]{4,3,2,1,0:T(8,128)(2,1)S(1)} copy-done((bf16[4,2,5,128,128]{4,3,2,1,0:T(8,128)(2,1)S(1)}, bf16[4,2,5,128,128]{4,3,2,1,0:T(8,128)(2,1)}, u32[]{:S(2)}) %copy-start) | copy-done | bytes 1310744
  1.9 0.0 copy-start.1
  2.0 0.9 %copy-done.1 = f32[32,4,2,128]{3,2,1,0:T(2,128)S(1)} copy-done((f32[32,4,2,128]{3,2,1,0:T(2,128)S(1)}, f32[32,4,2,128]{3,2,1,0:T(2,128)}, u32[]{:S(2)}) %copy-start.1) | copy-done | bytes 131096
  2.9 0.0 copy-start.2
  2.9 0.7 %copy-done.2 = s32[4,2,5]{2,1,0:T(2,128)S(1)} copy-done((s32[4,2,5]{2,1,0:T(2,128)S(1)}, s32[4,2,5]{2,1,0:T(2,128)}, u32[]{:S(2)}) %copy-start.2) | copy-done | bytes 184
  3.5 0.0 copy-start.3
  3.5 0.7 %copy-done.3 = f32[4,2,128]{2,1,0:T(2,128)S(1)} copy-done((f32[4,2,128]{2,1,0:T(2,128)S(1)}, f32[4,2,128]{2,1,0:T(2,128)}, u32[]{:S(2)}) %copy-start.3) | copy-done | bytes 4120
  4.2 55.0 %shard_map.76 = (f32[256,128]{1,0:T(8,128)S(1)}, f32[256,128]{1,0:T(8,128)S(1)}, f32[1]{0:T(128)}) custom-call(f32[256,128]{1,0:T(8,128)S(1)} %bitcast.7, bf16[1024,4096]{1,0:T(8,128)(2,1)} %bitcast.11, bf16[5120,128]{1,0:T(8,128)(2,1)S(1)} %bitcast.6, s32[4,2,5]{2,1,0:T(2,128)S(1)} %copy-done.2, f32[8,128]{1,0:T(8,128)S(1)} %bitcast.10), custom_call_target="tpu_custom_call" | custom-call | tf_op jit(solution)/shard_map/pallas_call | solution.py:345
  59.2 0.7 %copy.11 = f32[32,4,2,128]{3,2,1,0:T(2,128)} copy(f32[32,4,2,128]{3,2,1,0:T(2,128)S(1)} %bitcast.9) | data formatting | bytes 262144
  59.9 0.7 %copy.12 = f32[32,4,2,128]{3,2,1,0:T(2,128)} copy(f32[32,4,2,128]{3,2,1,0:T(2,128)S(1)} %bitcast.8) | data formatting | bytes 262144
Async XLA Ops:
  0.6 1.3 %copy-start = (bf16[4,2,5,128,128]{4,3,2,1,0:T(8,128)(2,1)S(1)}, bf16[4,2,5,128,128]{4,3,2,1,0:T(8,128)(2,1)}, u32[]{:S(2)}) copy-start(bf16[4,2,5,128,128]{4,3,2,1,0:T(8,128)(2,1)} %param.7) | copy-start | bytes 3932164
  1.9 0.9 %copy-start.1 = (f32[32,4,2,128]{3,2,1,0:T(2,128)S(1)}, f32[32,4,2,128]{3,2,1,0:T(2,128)}, u32[]{:S(2)}) copy-start(f32[32,4,2,128]{3,2,1,0:T(2,128)} %param.5) | copy-start | bytes 393220
  2.9 0.7 %copy-start.2 = (s32[4,2,5]{2,1,0:T(2,128)S(1)}, s32[4,2,5]{2,1,0:T(2,128)}, u32[]{:S(2)}) copy-start(s32[4,2,5]{2,1,0:T(2,128)} %mask_ref.1) | copy-start | bytes 484
  3.5 0.7 %copy-start.3 = (f32[4,2,128]{2,1,0:T(2,128)S(1)}, f32[4,2,128]{2,1,0:T(2,128)}, u32[]{:S(2)}) copy-start(f32[4,2,128]{2,1,0:T(2,128)} %param.9) | copy-start | bytes 12292

commit v2 on v1

--- a/solution.py
+++ b/solution.py
@@ -43,20 +43,19 @@
     return lax.dot_general(a, b, dims, precision=HIGH, preferred_element_type=F32)
 
 
-def eliminate(matrix, rights):
-    size = matrix.shape[0]
+def eliminate(systems):
+    size = systems[0][0].shape[0]
     sub = lax.broadcasted_iota(jnp.int32, (size, 1), 0)
     for k in range(size):
-        pivot = 1.0 / matrix[k : k + 1, k : k + 1]
-        column = matrix[:, k : k + 1]
-
-        def step(array):
-            row = array[k : k + 1, :] * pivot
-            return jnp.where(sub == k, row, array - column * row)
-
-        rights = [step(right) for right in rights]
-        matrix = step(matrix)
-    return rights
+        following = []
+        for matrix, right in systems:
+            pivot = 1.0 / matrix[k : k + 1, k : k + 1]
+            column = matrix[:, k : k + 1]
+            rows = [array[k : k + 1, :] * pivot for array in (matrix, right)]
+            following.append(tuple(
+                jnp.where(sub == k, row, array - column * row) for array, row in zip((matrix, right), rows)))
+        systems = following
+    return [right for _, right in systems]
 
 
 def kernel(dims, x_ref, f_hbm, b_hbm, mask_ref, nug_ref, sol_ref, rem_ref, grad_ref,
@@ -307,7 +306,9 @@
     w0, uu, small = finish(0, x0, y0, y0, state)
     g0 = small[:, :n]
     h0 = uu + small[:, n : 2 * n]
-    (s0,) = eliminate(h0, [g0])
+    eye = jnp.where(
+        lax.broadcasted_iota(jnp.int32, (n, n), 0) == lax.broadcasted_iota(jnp.int32, (n, n), 1), 1.0, 0.0)
+    s0, g0_inverse = eliminate([(h0, g0), (g0, eye)])
     r1 = x0 - high(s0, w0, TN)
     state = image(1, r1)
     y1 = state[0]
@@ -315,10 +316,10 @@
     g1 = small[:, :n]
     rar = low[:, n : 2 * n] + small[:, n : 2 * n]
     rav = low[:, :n] + small[:, 2 * n : 3 * n]
-    (m,) = eliminate(g0, [g1])
+    m = high(g0_inverse, g1, (((1,), (0,)), ((), ())))
     half = high(rav, m, (((1,), (0,)), ((), ())))
     h1 = rar + half + half.T + high(m, high(h0, m, (((1,), (0,)), ((), ()))), TN)
-    (s1,) = eliminate(h1, [g1])
+    (s1,) = eliminate([(h1, g1)])
     ms = high(m, s1, (((1,), (0,)), ((), ())))
     answer = high(s0 + ms, x0, TN) + high(s1, r1, TN)
     left = r1 - high(s1, t1, TN) - high(ms, w0, TN)
@@ -386,7 +387,7 @@
             dma((2, len(halo[0]))),
         ],
         compiler_params=pltpu.CompilerParams(
-            collective_id=0, has_side_effects=True, vmem_limit_bytes=48 * 1024 * 1024),
+            collective_id=0, has_side_effects=True, vmem_limit_bytes=63 * 1024 * 1024),
     )(
         probes.reshape(count * tiles, span),
         lowrank_factor.reshape(points, width),

time: 62.5 us -> 58.5 us (0.936)
  Pallas kernels: 55 us -> 52.8 us
  local copies, waits for them, and re-layouts: 4.9 us -> 3.14 us
    pallas_call x1, Pallas kernels: 55 us -> 52.8 us  [local(): pl.pallas_call(functools.partial(kernel, (nx, ny, rows, cols, count, widt...]
    unnamed x10 -> x2, local copies, waits for them, and re-layouts: 4.9 us -> 3.14 us
where the time goes in v2:
time: 58.5 us; the launch traced here: 58.3 us
  Pallas kernels  52.8 us (90%)
  local copies, waits for them, and re-layouts  3.14 us (5%)
  between operations  2.41 us (4%)
    pallas_call x1, Pallas kernels, local(): pl.pallas_call(functools.partial(kernel, (nx, ny, rows, cols, count, widt...  52.8 us
    unnamed x2, local copies, waits for them, and re-layouts  3.14 us

profile of v2, /device:TPU:0, one launch (start us, length us, event | category | flops | bytes accessed | tf_op | source)
XLA Modules:
  0.0 58.3 jit_solution(3564730215194783771)
XLA Ops:
  0.6 52.8 %shard_map.76 = (f32[256,128]{1,0:T(8,128)}, f32[256,128]{1,0:T(8,128)}, f32[1]{0:T(128)}) custom-call(f32[256,128]{1,0:T(8,128)} %bitcast.8, bf16[1024,4096]{1,0:T(8,128)(2,1)} %bitcast.6, bf16[5120,128]{1,0:T(8,128)(2,1)} %bitcast.7, s32[4,2,5]{2,1,0:T(2,128)} %mask_ref.1, f32[8,128]{1,0:T(8,128)} %bitcast.11), custom_call_target="tpu_custom_call" | custom-call | tf_op jit(solution)/shard_map/pallas_call | solution.py:346
  53.4 1.6 %copy.11 = f32[32,4,2,128]{3,2,1,0:T(2,128)} copy(f32[32,4,2,128]{3,2,1,0:T(2,128)} %bitcast.10) | data formatting | bytes 262144
  55.0 1.6 %copy.12 = f32[32,4,2,128]{3,2,1,0:T(2,128)} copy(f32[32,4,2,128]{3,2,1,0:T(2,128)} %bitcast.9) | data formatting | bytes 262144
